TPU v7x, 512 devices: a whole 4x4x16 slice. The times are simulated.
512 devices in a mesh: slab: 16 (over x, z_hi), chan: 32 (over z_lo, y, core).
Axes of the slice: x: 4, y: 4, z: 16 (z_hi: 4, z_lo: 4; z = z_hi * 4 + z_lo), core: 2. Of those that a mesh axis runs over, the one named last changes fastest.
Arguments:
- volume: bfloat16 [32, 512, 512], P('slab', 'chan'), may hold values from -6 to 6
- kernel: bfloat16 [27, 512, 512], P(None, 'chan'), may hold values from -0.0546875 to 0.0546875
- offset: float32 [512], P('chan'), may hold values from -3 to 3
- cotangent: bfloat16 [16, 512, 128], P('slab', 'chan'), may hold values from -6 to 6
Outputs:
- pooled: bfloat16 [16, 512, 128], P('slab', 'chan')
- volume_grad: bfloat16 [32, 512, 512], P('slab', 'chan')
All inputs are finite; a program needn't handle non-finite values.
Results may differ from a plain program's by a relative error of at most 0.02.
Values may be sent and summed in bfloat16 or wider, within the bound.
A program may use at most 64 MiB of HBM per device.

v0:
```python
import jax
import jax.numpy as jnp
from jax import lax
from jax.sharding import PartitionSpec as P

H = 16
W = 32


def extended(block, sides, width):
    for axis, dim in sides:
        count = lax.axis_size(axis)
        forward = [(i, i + 1) for i in range(count - 1)]
        backward = [(target, source) for source, target in forward]
        low = lax.ppermute(
            lax.slice_in_dim(block, block.shape[dim] - width, None, axis=dim), axis, forward
        )
        high = lax.ppermute(lax.slice_in_dim(block, 0, width, axis=dim), axis, backward)
        block = jnp.concatenate([low, block, high], axis=dim)
    return block


def shifted_plane(padded, kd, kh, kw):
    depth = padded.shape[0] - 2
    chans = padded.shape[1]
    grid = padded.reshape(depth + 2, chans, H, W)
    grid = jnp.pad(grid, ((0, 0), (0, 0), (1, 1), (1, 1)))
    return grid[kd : kd + depth, :, kh : kh + H, kw : kw + W].reshape(depth, chans, H * W)


def patch_columns(padded):
    depth = padded.shape[0] - 2
    pieces = []
    for kd in range(3):
        for kh in range(3):
            for kw in range(3):
                pieces.append(shifted_plane(padded, kd, kh, kw))
    stacked = jnp.stack(pieces, axis=1)
    return stacked.reshape(depth, 27 * padded.shape[1], H * W)


def shift_sum(products, chans):
    planes = products.shape[0]
    depth = planes - 2
    grid = products.reshape(planes, 27, chans, H, W)
    grid = jnp.pad(grid, ((0, 0), (0, 0), (0, 0), (1, 1), (1, 1)))
    total = jnp.zeros((depth, chans, H, W), jnp.float32)
    for kd in range(3):
        for kh in range(3):
            for kw in range(3):
                tap = 9 * kd + 3 * kh + kw
                total = total + grid[kd : kd + depth, tap, :, kh : kh + H, kw : kw + W]
    return total.reshape(depth, chans, H * W)


def per_device(volume, kernel, offset, cotangent):
    depth = volume.shape[0]
    in_local = volume.shape[1]
    out_local = offset.shape[0]
    out_all = kernel.shape[2]
    padded = extended(volume, (("slab", 0),), 1)
    columns = patch_columns(padded)
    flat_weights = kernel.reshape(27 * in_local, out_all)
    summed = lax.psum_scatter(
        jnp.einsum("dkp,ko->odp", columns, flat_weights, preferred_element_type=jnp.float32).astype(
            jnp.bfloat16
        ),
        "chan",
        scatter_dimension=0,
        tiled=True,
    ).astype(jnp.float32)
    preact = jnp.transpose(summed, (1, 0, 2))
    preact = preact + offset[None, :, None]
    active = jax.nn.silu(preact).reshape(depth // 2, 2, out_local, H // 2, 2, W // 2, 2)
    pooled = (
        jnp.mean(active, axis=(1, 4, 6))
        .reshape(depth // 2, out_local, H // 2 * (W // 2))
        .astype(jnp.bfloat16)
    )
    upper = (
        cotangent.astype(jnp.float32).reshape(depth // 2, 1, out_local, H // 2, 1, W // 2, 1) / 8.0
    )
    upper = jnp.broadcast_to(upper, (depth // 2, 2, out_local, H // 2, 2, W // 2, 2)).reshape(
        depth, out_local, H * W
    )
    sigma = jax.nn.sigmoid(preact)
    dpre = (upper * sigma * (1.0 + preact * (1.0 - sigma))).astype(jnp.bfloat16)
    flipped = kernel[::-1]
    gathered = lax.all_gather(dpre, "chan", axis=1, tiled=True)
    grad_pad = extended(gathered, (("slab", 0),), 1)
    all_weights = jnp.transpose(flipped, (2, 0, 1)).reshape(out_all, 27 * in_local)
    products = jnp.einsum("dop,ok->dkp", grad_pad, all_weights, preferred_element_type=jnp.float32)
    volume_grad = shift_sum(products, in_local)
    return (pooled, volume_grad.astype(jnp.bfloat16))


def solution(mesh):
    return jax.shard_map(
        per_device,
        mesh=mesh,
        in_specs=(
            P("slab", "chan", None),
            P(None, "chan", None),
            P("chan"),
            P("slab", "chan", None),
        ),
        out_specs=(P("slab", "chan", None), P("slab", "chan", None)),
        check_vma=False,
    )
```

profile of v0, /device:TPU:1, one launch (start us, length us, event | category | flops | bytes accessed | tf_op | source)
XLA Modules:
  0.0 485.8 jit_solution(183386575521747137)
XLA Ops:
  7.2 0.7 fusion.39
  8.0 9.6 %collective-permute-start = (bf16[1,16,512]{2,1,0:T(8,128)(2,1)S(1)}, bf16[1,16,512]{2,1,0:T(8,128)(2,1)S(1)}, u32[]{:S(2)}, u32[]{:S(2)}) collective-permute-start(bf16[1,16,512]{2,1,0:T(8,128)(2,1)S(1)} %get-tuple-element.51), channel_id=1, source_target_pairs={{0,32},{32,64},{64,96},{96,128},{128,160},{160,192},{192,224},{224... | collective-permute-start | bytes 49160 | tf_op jit(solution)/shard_map/ppermute | solution.py:15
  17.6 1.3 collective-permute-start.1
  18.9 0.8 copy.156
  19.7 7.8 %collective-permute-done.1 = bf16[1,16,512]{2,1,0:T(8,128)(2,1)S(1)} collective-permute-done((bf16[1,16,512]{2,1,0:T(8,128)(2,1)S(1)}, bf16[1,16,512]{2,1,0:T(8,128)(2,1)S(1)}, u32[]{:S(2)}, u32[]{:S(2)}) %collective-permute-start.1) | collective-permute-done | bytes 16416 | tf_op jit(solution)/shard_map/ppermute | solution.py:18
  27.5 0.8 pad_maximum_fusion
  28.3 0.2 reshape.120
  28.5 0.2 pad_slice_fusion.25
  28.8 0.8 pad_slice_fusion.24
  29.5 0.7 fusion.35
  30.3 0.7 copy.165
  30.9 0.7 copy.147
  31.7 0.1 stack_reshape.127
  31.9 0.1 stack_reshape.128
  32.0 0.1 stack_reshape.129
  32.1 0.1 stack_reshape.108
  32.3 0.1 stack_reshape.131
  32.4 0.1 stack_reshape.109
  32.5 0.1 stack_reshape.110
  32.8 0.1 stack_reshape.112
  32.9 0.1 stack_reshape.113
  33.1 0.1 stack_reshape.114
  33.2 0.1 stack_reshape.115
  33.3 0.1 stack_reshape.116
  33.5 0.1 stack_reshape.117
  33.6 0.1 stack_reshape.118
  33.7 0.1 stack_reshape.119
  33.9 0.1 stack_reshape.120
  34.0 0.1 stack_reshape.121
  34.1 0.1 stack_reshape.122
  34.3 0.1 stack_reshape.123
  34.4 0.1 stack_reshape.124
  34.5 0.1 stack_reshape.125
  34.6 0.1 stack_reshape.126
  34.8 4.2 stack.3
  39.1 0.8 fusion.9
  39.9 2.1 copy.171
  42.4 1.3 dynamic-slice
  44.4 285.8 %all-reduce.5.cloned.1.call-done = bf16[512,2,512]{2,1,0:T(2,128)(2,1)} async-done(((bf16[512,2,512]{2,1,0:T(2,128)(2,1)}), bf16[512,2,512]{2,1,0:T(2,128)(2,1)}) %all-reduce.5.cloned.1.call-update) | async-done | bytes 1048592
  330.2 0.8 constant_dynamic-slice_fusion
  331.1 0.6 copy.177
  331.7 64.6 %all-gather.2.cloned.1.call-done = bf16[2,512,512]{2,0,1:T(2,128)(2,1)} async-done(((bf16[2,16,512]{2,0,1:T(2,128)(2,1)}), bf16[2,512,512]{2,0,1:T(2,128)(2,1)}) %all-gather.2.cloned.1.call-update) | async-done | bytes 1048592 | tf_op jit(solution)/shard_map/all_gather | solution.py:89
  396.3 1.4 copy.178
  397.8 8.2 %collective-permute-start.2 = (bf16[1,512,512]{2,1,0:T(8,128)(2,1)S(1)}, bf16[1,512,512]{2,1,0:T(8,128)(2,1)}, u32[]{:S(2)}, u32[]{:S(2)}) collective-permute-start(bf16[1,512,512]{2,1,0:T(8,128)(2,1)S(1)} %get-tuple-element.21), channel_id=1, source_target_pairs={{0,32},{32,64},{64,96},{96,128},{128,160},{160,192},{192,224},{224... | collective-permute-start | bytes 1572872 | tf_op jit(solution)/shard_map/ppermute | solution.py:15
  406.0 1.3 collective-permute-start.3
  407.4 0.2 reduce_sum.18
  407.7 0.7 copy.181
  408.3 19.6 %collective-permute-done.2 = bf16[1,512,512]{2,1,0:T(8,128)(2,1)} collective-permute-done((bf16[1,512,512]{2,1,0:T(8,128)(2,1)S(1)}, bf16[1,512,512]{2,1,0:T(8,128)(2,1)}, u32[]{:S(2)}, u32[]{:S(2)}) %collective-permute-start.2) | collective-permute-done | bytes 524320 | tf_op jit(solution)/shard_map/ppermute | solution.py:15
  427.9 30.9 %collective-permute-done.3 = bf16[1,512,512]{2,1,0:T(8,128)(2,1)} collective-permute-done((bf16[1,512,512]{2,1,0:T(8,128)(2,1)S(1)}, bf16[1,512,512]{2,1,0:T(8,128)(2,1)}, u32[]{:S(2)}, u32[]{:S(2)}) %collective-permute-start.3) | collective-permute-done | bytes 524320 | tf_op jit(solution)/shard_map/ppermute | solution.py:18
  458.8 4.0 fusion.6
  462.9 9.5 %reshape.122 = f32[4,27,16,16,32]{4,3,2,1,0:T(8,128)} reshape(f32[4,432,512]{2,1,0:T(8,128)} %fusion.6) | data formatting | bytes 7077888 | tf_op jit(solution)/shard_map/reshape | solution.py:45
  472.4 4.3 pad_slice_fusion.8
  476.7 0.1 squeeze.83
  476.9 0.1 squeeze.85
  477.0 0.1 squeeze.86
  477.1 0.1 squeeze.87
  477.3 0.1 squeeze.89
  477.4 0.1 squeeze.90
  477.6 0.1 squeeze.91
  477.7 0.1 squeeze.92
  477.9 0.1 squeeze.88
  478.0 0.1 squeeze.84
  478.1 0.1 reshape.134
  478.3 0.7 add_convert_fusion
  (26 shorter events, 1.0 us)
Async XLA Ops:
  7.2 22.4 %copy-start = (bf16[2,16,512]{2,1,0:T(8,128)(2,1)S(1)}, bf16[2,16,512]{2,1,0:T(8,128)(2,1)}, u32[]{:S(2)}) copy-start(bf16[2,16,512]{2,1,0:T(8,128)(2,1)} %param.4) | copy-start | bytes 98308
  7.2 323.0 %all-reduce.5.cloned.1.call-start = ((), (), s32[]{:S(2)}) async-start(), calls=%async_computation.1 | async-start | bytes 2097152
  8.0 11.8 %collective-permute-start = (bf16[1,16,512]{2,1,0:T(8,128)(2,1)S(1)}, bf16[1,16,512]{2,1,0:T(8,128)(2,1)S(1)}, u32[]{:S(2)}, u32[]{:S(2)}) collective-permute-start(bf16[1,16,512]{2,1,0:T(8,128)(2,1)S(1)} %get-tuple-element.51), channel_id=1, source_target_pairs={{0,32},{32,64},{64,96},{96,128},{128,160},{160,192},{192,224},{224... | collective-permute-start | bytes 49160 | tf_op jit(solution)/shard_map/ppermute | solution.py:15
  17.6 9.9 %collective-permute-start.1 = (bf16[1,16,512]{2,1,0:T(8,128)(2,1)S(1)}, bf16[1,16,512]{2,1,0:T(8,128)(2,1)S(1)}, u32[]{:S(2)}, u32[]{:S(2)}) collective-permute-start(bf16[1,16,512]{2,1,0:T(8,128)(2,1)S(1)} %get-tuple-element.52), channel_id=1, source_target_pairs={{32,0},{64,32},{96,64},{128,96},{160,128},{192,160},{224,192},{256... | collective-permute-start | bytes 49160 | tf_op jit(solution)/shard_map/ppermute | solution.py:18
  27.5 0.8 copy-start.2
  32.7 6.4 %copy-start.1 = (bf16[27,16,512]{2,1,0:T(8,128)(2,1)S(1)}, bf16[27,16,512]{2,1,0:T(8,128)(2,1)}, u32[]{:S(2)}) copy-start(bf16[27,16,512]{2,1,0:T(8,128)(2,1)} %param.5) | copy-start | bytes 1327108
  39.0 3.1 copy-start.3
  39.0 291.9 %copy-start.4 = (f32[16]{0:T(128)S(1)}, f32[16]{0:T(128)}, u32[]{:S(2)}) copy-start(f32[16]{0:T(128)} %param.6) | copy-start | bytes 196
  42.0 354.3 %all-gather.2.cloned.1.call-start = ((), (), s32[]{:S(2)}) async-start(), calls=%async_computation | async-start | bytes 1081344 | tf_op jit(solution)/shard_map/all_gather | solution.py:89
  397.8 30.1 %collective-permute-start.2 = (bf16[1,512,512]{2,1,0:T(8,128)(2,1)S(1)}, bf16[1,512,512]{2,1,0:T(8,128)(2,1)}, u32[]{:S(2)}, u32[]{:S(2)}) collective-permute-start(bf16[1,512,512]{2,1,0:T(8,128)(2,1)S(1)} %get-tuple-element.21), channel_id=1, source_target_pairs={{0,32},{32,64},{64,96},{96,128},{128,160},{160,192},{192,224},{224... | collective-permute-start | bytes 1572872 | tf_op jit(solution)/shard_map/ppermute | solution.py:15
  406.0 52.8 %collective-permute-start.3 = (bf16[1,512,512]{2,1,0:T(8,128)(2,1)S(1)}, bf16[1,512,512]{2,1,0:T(8,128)(2,1)}, u32[]{:S(2)}, u32[]{:S(2)}) collective-permute-start(bf16[1,512,512]{2,1,0:T(8,128)(2,1)S(1)} %get-tuple-element.22), channel_id=1, source_target_pairs={{32,0},{64,32},{96,64},{128,96},{160,128},{192,160},{224,192},{256... | collective-permute-start | bytes 1572872 | tf_op jit(solution)/shard_map/ppermute | solution.py:18
Sparse Core Ops, SparseCore 0:
  42.2 287.9 all-reduce.4
  333.1 63.2 all-gather.1
where the time goes:
time: 487 us; the launch traced here: 486 us
  waiting for transfers between devices  409 us (84%)
  local copies, waits for them, and re-layouts  29.8 us (6%)
  starting transfers between devices  20.4 us (4%)
  between operations  15.1 us (3%)
  other arithmetic  6.83 us (1%)
    unnamed x3, waiting for transfers between devices  286 us
    all_gather x1, waiting for transfers between devices, per_device(): gathered = lax.all_gather(dpre, 'chan', axis=1, tiled=True)  64.6 us
    ppermute x2, waiting for transfers between devices, extended(): lax.ppermute(lax.slice_in_dim(block, 0, width, axis=dim), axis, backward)  38.7 us
    ppermute x2, waiting for transfers between devices, extended(): lax.ppermute(lax.slice_in_dim(block, block.shape[dim] - width, None, axis...  19.6 us
    ppermute x2, starting transfers between devices, extended(): lax.ppermute(lax.slice_in_dim(block, block.shape[dim] - width, None, axis...  17.8 us
  transfers between devices with their start and end apart: 6, of which 5 were waited for; matrix products, arithmetic and copies ran while one was open for 1% of the time, Pallas kernels for 0%

commit v1 on v0

v1 whole, which is shorter than its diff:
```python
import jax
import jax.numpy as jnp
from jax import lax
from jax.experimental import pallas as pl
from jax.experimental.pallas import tpu as pltpu
from jax.sharding import PartitionSpec as P

H = 16
W = 32
HW = H * W
ZN = 4
YN = 4
CHIPS = ZN * YN
MESH = pl.DeviceIdType.MESH
BF = jnp.bfloat16
F32 = jnp.float32


def iota(shape, dim):
    return lax.broadcasted_iota(jnp.int32, shape, dim)


def remote(src, dst, ssem, rsem, target):
    return pltpu.make_async_remote_copy(
        src_ref=src, dst_ref=dst, send_sem=ssem, recv_sem=rsem, device_id=target, device_id_type=MESH
    )


def in_grid(dh, dw):
    lane = iota((16, HW), 1)
    h, w = lane // W + dh, lane % W + dw
    return (h >= 0) & (h < H) & (w >= 0) & (w < W)


def moved(x, dh, dw):
    s = dh * W + dw
    if s == 0:
        return x
    return jnp.where(in_grid(dh, dw), pltpu.roll(x, (-s) % HW, 1), 0.0)


def dot(a, b):
    return jnp.dot(a, b, preferred_element_type=F32)


def body(
    vol_hbm, w_hbm, off_ref, cot_ref, pooled_ref, grad_ref,
    vbuf, wraw, wsend, wh, cols, acc, part, rs_recv, dp, hsend, hrecv, psend, precv,
    lsem, halo_s, halo_r, sib_s, sib_r, rs_s, rs_r, ag_s, ag_r, bh_s, bh_r, pair_s, pair_r,
):
    slab = lax.axis_index("slab")
    chan = lax.axis_index("chan")
    slabs = lax.axis_size("slab")
    core = chan % 2
    chip = chan // 2
    z, y = chip // YN, chip % YN
    up = lax.rem(slab + 1, slabs)
    down = lax.rem(slab + slabs - 1, slabs)
    sib = (slab, chan + 1 - 2 * core)

    def peer(other):
        return (slab, other * 2 + core)

    def near(s, b):
        return (s, chan if b == 0 else chan + 1 - 2 * core)

    load_v = pltpu.make_async_copy(vol_hbm, vbuf.at[pl.ds(1, 2), 0], lsem.at[0])
    load_w = pltpu.make_async_copy(w_hbm, wraw, lsem.at[1])
    load_v.start()
    load_w.start()
    barrier = pltpu.get_barrier_semaphore()
    pl.semaphore_signal(barrier, inc=1, device_id=sib, device_id_type=MESH)
    for s in (up, down):
        for b in range(2):
            pl.semaphore_signal(barrier, inc=1, device_id=near(s, b), device_id_type=MESH)

    def greet(d, _):
        pl.semaphore_signal(barrier, inc=1, device_id=peer(lax.rem(chip + d, CHIPS)), device_id_type=MESH)
        return 0

    lax.fori_loop(1, CHIPS, greet, 0)

    load_w.wait()
    wflat = wraw[...].reshape(432, 512)
    o = iota((512, 256), 0)
    r = iota((512, 256), 1)
    place = (r // 16) * 32 + r % 16
    pick_own = (o == place + 16 * core).astype(BF)
    pick_sib = (o == place + 16 * (1 - core)).astype(BF)
    wh[:, 0] = dot(wflat, pick_own).astype(BF).reshape(3, 144, 256)
    wsend[...] = dot(wflat, pick_sib).astype(BF).reshape(3, 144, 256)
    load_v.wait()

    pl.semaphore_wait(barrier, 5 + CHIPS - 1)

    halo = []
    for b in range(2):
        halo.append(remote(vbuf.at[2, 0], vbuf.at[0, b], halo_s.at[b], halo_r.at[b], near(up, b)))
        halo.append(remote(vbuf.at[1, 0], vbuf.at[3, b], halo_s.at[2 + b], halo_r.at[2 + b], near(down, b)))
    for c in halo:
        c.start()
    share_v = remote(vbuf.at[pl.ds(1, 2), 0], vbuf.at[pl.ds(1, 2), 1], sib_s.at[0], sib_r.at[0], sib)
    share_w = remote(wsend, wh.at[:, 1], sib_s.at[1], sib_r.at[1], sib)
    share_v.start()
    share_w.start()

    def columns(plane, b, keep=None):
        x = vbuf[plane, b].astype(F32)
        if keep is not None:
            x = jnp.where(keep, x, 0.0)
        for kh in range(3):
            for kw in range(3):
                row = b * 144 + (kh * 3 + kw) * 16
                cols[plane, row : row + 16] = moved(x, kh - 1, kw - 1).astype(BF)

    columns(1, 0)
    columns(2, 0)
    share_v.wait_recv()
    columns(1, 1)
    columns(2, 1)
    share_w.wait_recv()
    eye = (iota((256, 256), 0) == iota((256, 256), 1)).astype(BF)

    def turned(lo, hi):
        rows = wh[lo:hi].reshape((hi - lo) * 288, 256)
        return lax.dot_general(
            eye, rows, (((1,), (1,)), ((), ())), preferred_element_type=F32
        ).astype(BF)

    inner = cols[1:3].reshape(576, HW)
    acc[0] = dot(turned(1, 3), inner)
    acc[1] = dot(turned(0, 2), inner)
    w_lo = turned(0, 1)
    w_hi = turned(2, 3)

    for c in halo:
        c.wait_recv()
    for b in range(2):
        columns(0, b, slab > 0)
        columns(3, b, slab < slabs - 1)
    part[0] = (acc[0] + dot(w_lo, cols[0])).astype(BF)
    part[1] = (acc[1] + dot(w_hi, cols[3])).astype(BF)

    def rows(other):
        return pl.ds(pl.multiple_of(other * 16, 16), 16)

    def rs_copy(other, slot):
        return remote(part.at[:, rows(other)], rs_recv.at[slot], rs_s.at[other], rs_r.at[slot], peer(other))

    def ag_copy(other, slot):
        return remote(dp.at[:, rows(slot)], dp.at[:, rows(slot)], ag_s.at[other], ag_r.at[slot], peer(other))

    ztargets = (3 - z, lax.rem(z + 2, 4), z + 1 - 2 * lax.rem(z, 2), z)

    def spread(copy):
        for zi, zt in enumerate(ztargets):
            for dy in (2, 1, 3, 0):
                if zi < 3 or dy:
                    copy(zt * YN + lax.rem(y + dy, YN), chip).start()

    def collect(copy):
        def step(d, _):
            other = lax.rem(chip + d, CHIPS)
            copy(other, other).wait_recv()
            return 0

        lax.fori_loop(1, CHIPS, step, 0)

    def release(copy):
        def step(d, _):
            copy(lax.rem(chip + d, CHIPS), chip).wait_send()
            return 0

        lax.fori_loop(1, CHIPS, step, 0)

    spread(rs_copy)
    cell = iota((HW, 128), 0)
    coarse = iota((HW, 128), 1)
    pool = (coarse == (cell // (2 * W)) * (W // 2) + (cell % W) // 2).astype(BF)
    cell = iota((128, HW), 1)
    coarse = iota((128, HW), 0)
    unpool = (coarse == (cell // (2 * W)) * (W // 2) + (cell % W) // 2).astype(BF)
    upper = dot(cot_ref[0], unpool) * 0.125
    diag = iota((16, 16), 0) == iota((16, 16), 1)
    offset = jnp.sum(jnp.where(diag, jnp.broadcast_to(off_ref[...], (16, 16)), 0.0), axis=1, keepdims=True)
    total = part[:, rows(chip)].astype(F32)
    collect(rs_copy)

    def add(d, t):
        return t + rs_recv[lax.rem(chip + d, CHIPS)].astype(F32)

    total = lax.fori_loop(1, CHIPS, add, total)
    act = jnp.zeros((16, HW), F32)
    for d in range(2):
        v = total[d] + offset
        s = jax.nn.sigmoid(v)
        act = act + v * s
        dp[d, rows(chip)] = (upper * s * (1.0 + v * (1.0 - s))).astype(BF)
    spread(ag_copy)
    act_hi = act.astype(BF)
    act_lo = (act - act_hi.astype(F32)).astype(BF)
    pooled_ref[0] = ((dot(act_hi, pool) + dot(act_lo, pool)) * 0.125).astype(BF)
    collect(ag_copy)

    def gathered(prod):
        out = []
        for b in range(2):
            g = jnp.zeros((16, HW), F32)
            for kh in range(3):
                for kw in range(3):
                    row = b * 144 + (kh * 3 + kw) * 16
                    g = g + moved(prod[row : row + 16], 1 - kh, 1 - kw)
            out.append(g)
        return out

    flat = [wh[k].reshape(288, 256) for k in range(3)]
    dp0, dp1 = dp[0], dp[1]
    below = gathered(dot(flat[0], dp0))
    above = gathered(dot(flat[2], dp1))
    edge = []
    for b in range(2):
        hsend[0, b] = below[b].astype(BF)
        hsend[1, b] = above[b].astype(BF)
        edge.append(remote(hsend.at[0, b], hrecv.at[1, b], bh_s.at[b], bh_r.at[2 + b], near(down, b)))
        edge.append(remote(hsend.at[1, b], hrecv.at[0, b], bh_s.at[2 + b], bh_r.at[b], near(up, b)))
    for c in edge:
        c.start()
    g0 = gathered(dot(flat[0], dp1) + dot(flat[1], dp0))
    g1 = gathered(dot(flat[1], dp1) + dot(flat[2], dp0))
    psend[0] = g0[1].astype(BF)
    psend[1] = g1[1].astype(BF)
    pair = remote(psend, precv, pair_s, pair_r, sib)
    pair.start()
    pair.wait_recv()
    g0 = g0[0] + precv[0].astype(F32)
    g1 = g1[0] + precv[1].astype(F32)
    for c in edge:
        c.wait_recv()
    from_down = hrecv[0, 0].astype(F32) + hrecv[0, 1].astype(F32)
    from_up = hrecv[1, 0].astype(F32) + hrecv[1, 1].astype(F32)
    grad_ref[0] = (g0 + jnp.where(slab > 0, from_down, 0.0)).astype(BF)
    grad_ref[1] = (g1 + jnp.where(slab < slabs - 1, from_up, 0.0)).astype(BF)

    for c in halo + [share_v, share_w, pair] + edge:
        c.wait_send()
    release(rs_copy)
    release(ag_copy)


def per_device(volume, kernel, offset, cotangent):
    vmem = pl.BlockSpec(memory_space=pltpu.VMEM)
    hbm = pl.BlockSpec(memory_space=pl.ANY)
    dma = pltpu.SemaphoreType.DMA
    return pl.pallas_call(
        body,
        out_shape=(
            jax.ShapeDtypeStruct((1, 16, HW // 4), BF),
            jax.ShapeDtypeStruct((2, 16, HW), BF),
        ),
        in_specs=[hbm, hbm, vmem, vmem],
        out_specs=(vmem, vmem),
        scratch_shapes=[
            pltpu.VMEM((4, 2, 16, HW), BF),
            pltpu.VMEM((27, 16, 512), BF),
            pltpu.VMEM((3, 144, 256), BF),
            pltpu.VMEM((3, 2, 144, 256), BF),
            pltpu.VMEM((4, 288, HW), BF),
            pltpu.VMEM((2, 256, HW), F32),
            pltpu.VMEM((2, 256, HW), BF),
            pltpu.VMEM((CHIPS, 2, 16, HW), BF),
            pltpu.VMEM((2, 256, HW), BF),
            pltpu.VMEM((2, 2, 16, HW), BF),
            pltpu.VMEM((2, 2, 16, HW), BF),
            pltpu.VMEM((2, 16, HW), BF),
            pltpu.VMEM((2, 16, HW), BF),
            dma((2,)), dma((4,)), dma((4,)), dma((2,)), dma((2,)),
            dma((CHIPS,)), dma((CHIPS,)), dma((CHIPS,)), dma((CHIPS,)),
            dma((4,)), dma((4,)), dma, dma,
        ],
        compiler_params=pltpu.CompilerParams(
            collective_id=0, has_side_effects=True, vmem_limit_bytes=40 * 2**20
        ),
        name="conv_level",
    )(volume, kernel, offset.reshape(1, 16), cotangent)


def solution(mesh):
    return jax.shard_map(
        per_device,
        mesh=mesh,
        in_specs=(
            P("slab", "chan", None),
            P(None, "chan", None),
            P("chan"),
            P("slab", "chan", None),
        ),
        out_specs=(P("slab", "chan", None), P("slab", "chan", None)),
        check_vma=False,
    )
```

time: 487 us -> 62.7 us (0.13)
  waiting for transfers between devices: 409 us -> 0 us
  Pallas kernels: 0 us -> 57.4 us
  local copies, waits for them, and re-layouts: 29.8 us -> 4.31 us
  starting transfers between devices: 20.4 us -> 0 us
  between operations: 15.1 us -> 0.65 us
  other arithmetic: 6.83 us -> 0 us
    unnamed x3 -> x0, waiting for transfers between devices: 286 us -> none
    all_gather x1 -> x0, waiting for transfers between devices: 64.6 us -> none  [per_device(): gathered = lax.all_gather(dpre, 'chan', axis=1, tiled=True)]
    ppermute x4 -> x0, waiting for transfers between devices: 58.3 us -> none  [the longest x2 38.7 us: extended(): lax.ppermute(lax.slice_in_dim(block, 0, width, axis=dim), axis, backward)]
    pallas_call x0 -> x1, Pallas kernels: none -> 57.4 us  [per_device(): pl.pallas_call(body, out_shape=(jax.ShapeDtypeStruct((1, 16, HW // 4), BF...]
    ppermute x4 -> x0, starting transfers between devices: 20.4 us -> none  [the longest x2 17.8 us: extended(): lax.ppermute(lax.slice_in_dim(block, block.shape[dim] - width, None, axis...]
    reshape x2 -> x0, local copies, waits for them, and re-layouts: 9.72 us -> none  [the longest x1 9.54 us: shift_sum(): grid = products.reshape(planes, 27, chans, H, W)]
    another operation x28 -> x0, local copies, waits for them, and re-layouts: 9.36 us -> none  [patch_columns(): stacked = jnp.stack(pieces, axis=1)]
  transfers between devices with their start and end apart: 6 -> 0, of which waited for: 5 -> 0; matrix products, arithmetic and copies ran while one was open for 1% -> 0% of each run, Pallas kernels for 0% -> 0%
where the time goes in v1:
time: 62.7 us; the launch traced here: 62.4 us
  Pallas kernels  57.4 us (92%)
  local copies, waits for them, and re-layouts  4.31 us (7%)
  between operations  0.65 us (1%)
    pallas_call x1, Pallas kernels, per_device(): pl.pallas_call(body, out_shape=(jax.ShapeDtypeStruct((1, 16, HW // 4), BF...  57.4 us
    unnamed x10, local copies, waits for them, and re-layouts  4.31 us

profile of v1, /device:TPU:1, one launch (start us, length us, event | category | flops | bytes accessed | tf_op | source)
XLA Modules:
  0.0 62.4 jit_solution(10264109577318690121)
XLA Ops:
  0.6 0.0 copy-start.3
  0.6 0.6 %copy-done.3 = f32[16]{0:T(128)S(1)} copy-done((f32[16]{0:T(128)S(1)}, f32[16]{0:T(128)}, u32[]{:S(2)}) %copy-start.3) | copy-done | bytes 88
  1.3 0.0 copy-start
  1.3 1.0 %copy-done = bf16[27,16,512]{2,1,0:T(8,128)(2,1)S(1)} copy-done((bf16[27,16,512]{2,1,0:T(8,128)(2,1)S(1)}, bf16[27,16,512]{2,1,0:T(8,128)(2,1)}, u32[]{:S(2)}) %copy-start) | copy-done | bytes 442392
  2.3 0.0 copy-start.1
  2.3 0.8 %copy-done.1 = bf16[2,16,512]{2,1,0:T(8,128)(2,1)S(1)} copy-done((bf16[2,16,512]{2,1,0:T(8,128)(2,1)S(1)}, bf16[2,16,512]{2,1,0:T(8,128)(2,1)}, u32[]{:S(2)}) %copy-start.1) | copy-done | bytes 32792
  3.1 0.0 copy-start.2
  3.1 0.7 %copy-done.2 = bf16[1,16,128]{2,1,0:T(8,128)(2,1)S(1)} copy-done((bf16[1,16,128]{2,1,0:T(8,128)(2,1)S(1)}, bf16[1,16,128]{2,1,0:T(8,128)(2,1)}, u32[]{:S(2)}) %copy-start.2) | copy-done | bytes 4120
  3.7 57.4 %conv_level.1 = (bf16[1,16,128]{2,1,0:T(8,128)(2,1)S(1)}, bf16[2,16,512]{2,1,0:T(8,128)(2,1)S(1)}) custom-call(bf16[2,16,512]{2,1,0:T(8,128)(2,1)S(1)} %copy-done.1, bf16[27,16,512]{2,1,0:T(8,128)(2,1)S(1)} %copy-done, f32[1,16]{1,0:T(1,128)S(1)} %bitcast.1, bf16[1,16,128]{2,1,0:T(8,128)(2,1)S(1)} %copy-done.2), custom_call_target="tpu_custom_call" | custom-call | tf_op jit(solution)/shard_map/conv_level/pallas_call | solution.py:254
  61.2 0.6 copy.8
  61.8 0.6 copy.9
Async XLA Ops:
  0.6 0.7 %copy-start.3 = (f32[16]{0:T(128)S(1)}, f32[16]{0:T(128)}, u32[]{:S(2)}) copy-start(f32[16]{0:T(128)} %param.6) | copy-start | bytes 196
  1.3 1.0 %copy-start = (bf16[27,16,512]{2,1,0:T(8,128)(2,1)S(1)}, bf16[27,16,512]{2,1,0:T(8,128)(2,1)}, u32[]{:S(2)}) copy-start(bf16[27,16,512]{2,1,0:T(8,128)(2,1)} %w_hbm.1) | copy-start | bytes 1327108
  2.3 0.8 %copy-start.1 = (bf16[2,16,512]{2,1,0:T(8,128)(2,1)S(1)}, bf16[2,16,512]{2,1,0:T(8,128)(2,1)}, u32[]{:S(2)}) copy-start(bf16[2,16,512]{2,1,0:T(8,128)(2,1)} %vol_hbm.1) | copy-start | bytes 98308
  3.1 0.7 %copy-start.2 = (bf16[1,16,128]{2,1,0:T(8,128)(2,1)S(1)}, bf16[1,16,128]{2,1,0:T(8,128)(2,1)}, u32[]{:S(2)}) copy-start(bf16[1,16,128]{2,1,0:T(8,128)(2,1)} %cot_ref.1) | copy-start | bytes 12292

commit v2 on v1

--- a/solution.py
+++ b/solution.py
@@ -8,9 +8,7 @@
 H = 16
 W = 32
 HW = H * W
-ZN = 4
 YN = 4
-CHIPS = ZN * YN
 MESH = pl.DeviceIdType.MESH
 BF = jnp.bfloat16
 F32 = jnp.float32
@@ -44,22 +42,26 @@
 
 
 def body(
-    vol_hbm, w_hbm, off_ref, cot_ref, pooled_ref, grad_ref,
-    vbuf, wraw, wsend, wh, cols, acc, part, rs_recv, dp, hsend, hrecv, psend, precv,
-    lsem, halo_s, halo_r, sib_s, sib_r, rs_s, rs_r, ag_s, ag_r, bh_s, bh_r, pair_s, pair_r,
+    vol_hbm, w_hbm, off_hbm, cot_hbm, pooled_ref, grad_ref,
+    vbuf, wraw, off_ref, cot_ref, wsend, wh, cols, acc, part, ysum, zsend, zsum, dp, hsend, hrecv, psend, precv,
+    lsem, halo_s, halo_r, sib_s, sib_r, ry_s, ry_r, rz_s, rz_r, az_s, az_r, ay_s, ay_r, bh_s, bh_r, pair_s, pair_r,
 ):
     slab = lax.axis_index("slab")
     chan = lax.axis_index("chan")
     slabs = lax.axis_size("slab")
     core = chan % 2
-    chip = chan // 2
-    z, y = chip // YN, chip % YN
+    z, y = chan // 2 // YN, chan // 2 % YN
     up = lax.rem(slab + 1, slabs)
     down = lax.rem(slab + slabs - 1, slabs)
     sib = (slab, chan + 1 - 2 * core)
 
-    def peer(other):
-        return (slab, other * 2 + core)
+    zs = (z, z + 1 - 2 * lax.rem(z, 2), lax.rem(z + 2, 4), 3 - z)
+
+    def yto(dy):
+        return (slab, (z * YN + lax.rem(y + dy, YN)) * 2 + core)
+
+    def zto(dz):
+        return (slab, (zs[dz] * YN + y) * 2 + core)
 
     def near(s, b):
         return (s, chan if b == 0 else chan + 1 - 2 * core)
@@ -68,30 +70,33 @@
     load_w = pltpu.make_async_copy(w_hbm, wraw, lsem.at[1])
     load_v.start()
     load_w.start()
+    load_o = pltpu.make_async_copy(off_hbm, off_ref, lsem.at[2])
+    load_c = pltpu.make_async_copy(cot_hbm, cot_ref, lsem.at[3])
+    load_o.start()
+    load_c.start()
     barrier = pltpu.get_barrier_semaphore()
     pl.semaphore_signal(barrier, inc=1, device_id=sib, device_id_type=MESH)
     for s in (up, down):
         for b in range(2):
             pl.semaphore_signal(barrier, inc=1, device_id=near(s, b), device_id_type=MESH)
 
-    def greet(d, _):
-        pl.semaphore_signal(barrier, inc=1, device_id=peer(lax.rem(chip + d, CHIPS)), device_id_type=MESH)
-        return 0
-
-    lax.fori_loop(1, CHIPS, greet, 0)
+    for d in range(1, 4):
+        pl.semaphore_signal(barrier, inc=1, device_id=zto(d), device_id_type=MESH)
+        pl.semaphore_signal(barrier, inc=1, device_id=yto(d), device_id_type=MESH)
 
     load_w.wait()
     wflat = wraw[...].reshape(432, 512)
     o = iota((512, 256), 0)
     r = iota((512, 256), 1)
-    place = (r // 16) * 32 + r % 16
+    zt = 2 * ((z // 2 + r // 128) % 2) + (z % 2 + r // 64) % 2
+    place = (zt * YN + r // 16 % YN) * 32 + r % 16
     pick_own = (o == place + 16 * core).astype(BF)
     pick_sib = (o == place + 16 * (1 - core)).astype(BF)
     wh[:, 0] = dot(wflat, pick_own).astype(BF).reshape(3, 144, 256)
     wsend[...] = dot(wflat, pick_sib).astype(BF).reshape(3, 144, 256)
     load_v.wait()
 
-    pl.semaphore_wait(barrier, 5 + CHIPS - 1)
+    pl.semaphore_wait(barrier, 11)
 
     halo = []
     for b in range(2):
@@ -141,66 +146,77 @@
     part[0] = (acc[0] + dot(w_lo, cols[0])).astype(BF)
     part[1] = (acc[1] + dot(w_hi, cols[3])).astype(BF)
 
-    def rows(other):
-        return pl.ds(pl.multiple_of(other * 16, 16), 16)
-
-    def rs_copy(other, slot):
-        return remote(part.at[:, rows(other)], rs_recv.at[slot], rs_s.at[other], rs_r.at[slot], peer(other))
-
-    def ag_copy(other, slot):
-        return remote(dp.at[:, rows(slot)], dp.at[:, rows(slot)], ag_s.at[other], ag_r.at[slot], peer(other))
-
-    ztargets = (3 - z, lax.rem(z + 2, 4), z + 1 - 2 * lax.rem(z, 2), z)
-
-    def spread(copy):
-        for zi, zt in enumerate(ztargets):
-            for dy in (2, 1, 3, 0):
-                if zi < 3 or dy:
-                    copy(zt * YN + lax.rem(y + dy, YN), chip).start()
-
-    def collect(copy):
-        def step(d, _):
-            other = lax.rem(chip + d, CHIPS)
-            copy(other, other).wait_recv()
-            return 0
-
-        lax.fori_loop(1, CHIPS, step, 0)
-
-    def release(copy):
-        def step(d, _):
-            copy(lax.rem(chip + d, CHIPS), chip).wait_send()
-            return 0
-
-        lax.fori_loop(1, CHIPS, step, 0)
-
-    spread(rs_copy)
+    def rows(dz, yt):
+        return pl.ds(pl.multiple_of(dz * 64 + yt * 16, 16), 16)
+
+    def ry(dz, dy):
+        k = dz * 4 + dy
+        return remote(part.at[:, rows(dz, lax.rem(y + dy, YN))], ysum.at[dz, dy], ry_s.at[k], ry_r.at[k], yto(dy))
+
+    def rz(dz):
+        return remote(zsend.at[dz], zsum.at[dz], rz_s.at[dz], rz_r.at[dz], zto(dz))
+
+    def az(dz):
+        return remote(dp.at[:, rows(0, y)], dp.at[:, rows(dz, y)], az_s.at[dz], az_r.at[dz], zto(dz))
+
+    def ay(dz, dy):
+        k = dz * 4 + dy
+        return remote(dp.at[:, rows(dz, y)], dp.at[:, rows(dz, y)], ay_s.at[k], ay_r.at[k], yto(dy))
+
+    def ay_arrival(dz, dy):
+        k = dz * 4 + dy
+        here = rows(dz, lax.rem(y + 4 - dy, YN))
+        return remote(dp.at[:, here], dp.at[:, here], ay_s.at[k], ay_r.at[k], yto(dy))
+
+    for dz in (3, 2, 1, 0):
+        for dy in (2, 1, 3):
+            ry(dz, dy).start()
     cell = iota((HW, 128), 0)
     coarse = iota((HW, 128), 1)
     pool = (coarse == (cell // (2 * W)) * (W // 2) + (cell % W) // 2).astype(BF)
     cell = iota((128, HW), 1)
     coarse = iota((128, HW), 0)
     unpool = (coarse == (cell // (2 * W)) * (W // 2) + (cell % W) // 2).astype(BF)
+    load_o.wait()
+    load_c.wait()
     upper = dot(cot_ref[0], unpool) * 0.125
     diag = iota((16, 16), 0) == iota((16, 16), 1)
     offset = jnp.sum(jnp.where(diag, jnp.broadcast_to(off_ref[...], (16, 16)), 0.0), axis=1, keepdims=True)
-    total = part[:, rows(chip)].astype(F32)
-    collect(rs_copy)
-
-    def add(d, t):
-        return t + rs_recv[lax.rem(chip + d, CHIPS)].astype(F32)
-
-    total = lax.fori_loop(1, CHIPS, add, total)
+    def ytotal(dz):
+        t = part[:, rows(dz, y)].astype(F32)
+        for dy in (1, 2, 3):
+            ry(dz, dy).wait_recv()
+        for dy in (1, 2, 3):
+            t = t + ysum[dz, dy].astype(F32)
+        return t
+
+    for dz in (3, 2, 1):
+        zsend[dz] = ytotal(dz).astype(BF)
+        rz(dz).start()
+    total = ytotal(0)
+    for dz in (1, 2, 3):
+        rz(dz).wait_recv()
+        total = total + zsum[dz].astype(F32)
     act = jnp.zeros((16, HW), F32)
     for d in range(2):
         v = total[d] + offset
         s = jax.nn.sigmoid(v)
         act = act + v * s
-        dp[d, rows(chip)] = (upper * s * (1.0 + v * (1.0 - s))).astype(BF)
-    spread(ag_copy)
+        dp[d, rows(0, y)] = (upper * s * (1.0 + v * (1.0 - s))).astype(BF)
+    for dz in (3, 2, 1):
+        az(dz).start()
+    for dy in (2, 1, 3):
+        ay(0, dy).start()
     act_hi = act.astype(BF)
     act_lo = (act - act_hi.astype(F32)).astype(BF)
     pooled_ref[0] = ((dot(act_hi, pool) + dot(act_lo, pool)) * 0.125).astype(BF)
-    collect(ag_copy)
+    for dz in (1, 2, 3):
+        az(dz).wait_recv()
+        for dy in (2, 1, 3):
+            ay(dz, dy).start()
+    for dz in range(4):
+        for dy in (1, 2, 3):
+            ay_arrival(dz, dy).wait_recv()
 
     def gathered(prod):
         out = []
@@ -243,8 +259,13 @@
 
     for c in halo + [share_v, share_w, pair] + edge:
         c.wait_send()
-    release(rs_copy)
-    release(ag_copy)
+    for dz in range(4):
+        for dy in (1, 2, 3):
+            ry(dz, dy).wait_send()
+            ay(dz, dy).wait_send()
+    for dz in (1, 2, 3):
+        rz(dz).wait_send()
+        az(dz).wait_send()
 
 
 def per_device(volume, kernel, offset, cotangent):
@@ -257,31 +278,36 @@
             jax.ShapeDtypeStruct((1, 16, HW // 4), BF),
             jax.ShapeDtypeStruct((2, 16, HW), BF),
         ),
-        in_specs=[hbm, hbm, vmem, vmem],
+        in_specs=[hbm] * 4,
         out_specs=(vmem, vmem),
         scratch_shapes=[
             pltpu.VMEM((4, 2, 16, HW), BF),
             pltpu.VMEM((27, 16, 512), BF),
+            pltpu.VMEM((1, 16), F32),
+            pltpu.VMEM((1, 16, HW // 4), BF),
             pltpu.VMEM((3, 144, 256), BF),
             pltpu.VMEM((3, 2, 144, 256), BF),
             pltpu.VMEM((4, 288, HW), BF),
             pltpu.VMEM((2, 256, HW), F32),
             pltpu.VMEM((2, 256, HW), BF),
-            pltpu.VMEM((CHIPS, 2, 16, HW), BF),
+            pltpu.VMEM((4, 4, 2, 16, HW), BF),
+            pltpu.VMEM((4, 2, 16, HW), BF),
+            pltpu.VMEM((4, 2, 16, HW), BF),
             pltpu.VMEM((2, 256, HW), BF),
             pltpu.VMEM((2, 2, 16, HW), BF),
             pltpu.VMEM((2, 2, 16, HW), BF),
             pltpu.VMEM((2, 16, HW), BF),
             pltpu.VMEM((2, 16, HW), BF),
-            dma((2,)), dma((4,)), dma((4,)), dma((2,)), dma((2,)),
-            dma((CHIPS,)), dma((CHIPS,)), dma((CHIPS,)), dma((CHIPS,)),
+            dma((4,)), dma((4,)), dma((4,)), dma((2,)), dma((2,)),
+            dma((16,)), dma((16,)), dma((4,)), dma((4,)),
+            dma((4,)), dma((4,)), dma((16,)), dma((16,)),
             dma((4,)), dma((4,)), dma, dma,
         ],
         compiler_params=pltpu.CompilerParams(
             collective_id=0, has_side_effects=True, vmem_limit_bytes=40 * 2**20
         ),
         name="conv_level",
-    )(volume, kernel, offset.reshape(1, 16), cotangent)
+    )(*(pltpu.with_memory_space_constraint(a, pltpu.HBM) for a in (volume, kernel, offset.reshape(1, 16), cotangent)))
 
 
 def solution(mesh):

time: 62.7 us -> 52.7 us (0.84)
  Pallas kernels: 57.4 us -> 50.8 us
  local copies, waits for them, and re-layouts: 4.31 us -> 1.21 us
    pallas_call x1, Pallas kernels: 57.4 us -> 50.8 us  [per_device(): pl.pallas_call(body, out_shape=(jax.ShapeDtypeStruct((1, 16, HW // 4), BF...]
    unnamed x10 -> x2, local copies, waits for them, and re-layouts: 4.31 us -> 1.21 us
where the time goes in v2:
time: 52.7 us; the launch traced here: 52.6 us
  Pallas kernels  50.8 us (96%)
  local copies, waits for them, and re-layouts  1.21 us (2%)
  between operations  0.64 us (1%)
    pallas_call x1, Pallas kernels, per_device(): pl.pallas_call(body, out_shape=(jax.ShapeDtypeStruct((1, 16, HW // 4), BF...  50.8 us
    unnamed x2, local copies, waits for them, and re-layouts  1.21 us

profile of v2, /device:TPU:1, one launch (start us, length us, event | category | flops | bytes accessed | tf_op | source)
XLA Modules:
  0.0 52.6 jit_solution(12006159597628277862)
XLA Ops:
  0.6 50.8 %conv_level.1 = (bf16[1,16,128]{2,1,0:T(8,128)(2,1)S(1)}, bf16[2,16,512]{2,1,0:T(8,128)(2,1)S(1)}) custom-call(bf16[2,16,512]{2,1,0:T(8,128)(2,1)} %vol_hbm.1, bf16[27,16,512]{2,1,0:T(8,128)(2,1)} %w_hbm.1, f32[1,16]{1,0:T(1,128)} %bitcast.1, bf16[1,16,128]{2,1,0:T(8,128)(2,1)} %cot_hbm.1), custom_call_target="tpu_custom_call" | custom-call | tf_op jit(solution)/shard_map/conv_level/pallas_call | solution.py:275
  51.4 0.6 %copy.8 = bf16[1,16,128]{2,1,0:T(8,128)(2,1)} copy(bf16[1,16,128]{2,1,0:T(8,128)(2,1)S(1)} %get-tuple-element.4) | data formatting | bytes 8192
  52.0 0.6 %copy.9 = bf16[2,16,512]{2,1,0:T(8,128)(2,1)} copy(bf16[2,16,512]{2,1,0:T(8,128)(2,1)S(1)} %get-tuple-element.5) | data formatting | bytes 65536

commit v3 on v2

v3 whole, which is shorter than its diff:
```python
import jax
import jax.numpy as jnp
from jax import lax
from jax.experimental import pallas as pl
from jax.experimental.pallas import tpu as pltpu
from jax.sharding import PartitionSpec as P

H = 16
W = 32
HW = H * W
YN = 4
MESH = pl.DeviceIdType.MESH
BF = jnp.bfloat16
F32 = jnp.float32


def iota(shape, dim):
    return lax.broadcasted_iota(jnp.int32, shape, dim)


def remote(src, dst, ssem, rsem, target):
    return pltpu.make_async_remote_copy(
        src_ref=src, dst_ref=dst, send_sem=ssem, recv_sem=rsem, device_id=target, device_id_type=MESH
    )


def in_grid(dh, dw):
    lane = iota((16, HW), 1)
    h, w = lane // W + dh, lane % W + dw
    return (h >= 0) & (h < H) & (w >= 0) & (w < W)


def moved(x, dh, dw):
    s = dh * W + dw
    if s == 0:
        return x
    return jnp.where(in_grid(dh, dw), pltpu.roll(x, (-s) % HW, 1), 0.0)


def dot(a, b):
    return jnp.dot(a, b, preferred_element_type=F32)


def body(
    vol_hbm, w_hbm, off_hbm, cot_hbm, pooled_ref, grad_ref,
    vbuf, wraw, wturn, off_ref, cot_ref, wsend, wh, cols, acc, part, ysum, zsend, zsum, dp, hsend, hrecv, psend, precv,
    lsem, halo_s, halo_r, sib_s, sib_r, ry_s, ry_r, rz_s, rz_r, az_s, az_r, ay_s, ay_r, bh_s, bh_r, pair_s, pair_r,
):
    slab = lax.axis_index("slab")
    chan = lax.axis_index("chan")
    slabs = lax.axis_size("slab")
    core = chan % 2
    z, y = chan // 2 // YN, chan // 2 % YN
    up = lax.rem(slab + 1, slabs)
    down = lax.rem(slab + slabs - 1, slabs)
    sib = (slab, chan + 1 - 2 * core)

    zs = (z, z + 1 - 2 * lax.rem(z, 2), lax.rem(z + 2, 4), 3 - z)

    first = lax.rem(slab, 4) // 3
    second = 1 - first
    planes = (first, second)

    def yto(dy):
        return (slab, (z * YN + lax.rem(y + dy, YN)) * 2 + core)

    def zto(dz):
        return (slab, (zs[dz] * YN + y) * 2 + core)

    def near(s, b):
        return (s, chan if b == 0 else chan + 1 - 2 * core)

    barrier = pltpu.get_barrier_semaphore()
    pl.semaphore_signal(barrier, inc=1, device_id=sib, device_id_type=MESH)
    for s in (up, down):
        for b in range(2):
            pl.semaphore_signal(barrier, inc=1, device_id=near(s, b), device_id_type=MESH)

    for d in range(1, 4):
        pl.semaphore_signal(barrier, inc=1, device_id=zto(d), device_id_type=MESH)
        pl.semaphore_signal(barrier, inc=1, device_id=yto(d), device_id_type=MESH)

    load_v = pltpu.make_async_copy(vol_hbm, vbuf.at[pl.ds(1, 2), 0], lsem.at[0])
    load_w = pltpu.make_async_copy(w_hbm, wraw, lsem.at[1])
    load_v.start()
    load_w.start()
    load_o = pltpu.make_async_copy(off_hbm, off_ref, lsem.at[2])
    load_c = pltpu.make_async_copy(cot_hbm, cot_ref, lsem.at[3])
    load_o.start()
    load_c.start()
    pl.semaphore_wait(barrier, 11)

    halo = []
    for b in range(2):
        halo.append(remote(vol_hbm.at[1], vbuf.at[0, b], halo_s.at[b], halo_r.at[b], near(up, b)))
        halo.append(remote(vol_hbm.at[0], vbuf.at[3, b], halo_s.at[2 + b], halo_r.at[2 + b], near(down, b)))
    for c in halo:
        c.start()
    share_v = remote(vol_hbm, vbuf.at[pl.ds(1, 2), 1], sib_s.at[0], sib_r.at[0], sib)
    share_w = remote(wsend, wh.at[:, 1], sib_s.at[1], sib_r.at[1], sib)
    share_v.start()

    load_w.wait()
    wflat = wraw[...].reshape(432, 512)
    o = iota((512, 256), 0)
    r = iota((512, 256), 1)
    zt = 2 * ((z // 2 + r // 128) % 2) + (z % 2 + r // 64) % 2
    place = o - (zt * YN + r // 16 % YN) * 32 - r % 16
    wsend[...] = dot(wflat, (place == 16 * (1 - core)).astype(BF)).astype(BF).reshape(3, 144, 256)
    share_w.start()
    wh[:, 0] = dot(wflat, (place == 16 * core).astype(BF)).astype(BF).reshape(3, 144, 256)
    load_v.wait()

    def columns(plane, b, keep=None):
        x = vbuf[plane, b].astype(F32)
        if keep is not None:
            x = jnp.where(keep, x, 0.0)
        for kh in range(3):
            for kw in range(3):
                row = b * 144 + (kh * 3 + kw) * 16
                cols[plane, row : row + 16] = moved(x, kh - 1, kw - 1).astype(BF)

    columns(1, 0)
    columns(2, 0)
    share_v.wait_recv()
    columns(1, 1)
    columns(2, 1)
    share_w.wait_recv()
    eye = (iota((256, 256), 0) == iota((256, 256), 1)).astype(BF)

    def turned(lo, hi):
        rows = wh[lo:hi].reshape((hi - lo) * 288, 256)
        return lax.dot_general(
            eye, rows, (((1,), (1,)), ((), ())), preferred_element_type=F32
        ).astype(BF)

    inner = cols[1:3].reshape(576, HW)
    acc[0] = dot(turned(1, 3), inner)
    acc[1] = dot(turned(0, 2), inner)
    wturn[0] = turned(0, 1)
    wturn[1] = turned(2, 3)

    def rows(dz, yt):
        return pl.ds(pl.multiple_of(dz * 64 + yt * 16, 16), 16)

    def ry(p, dz, dy):
        k = dz * 4 + dy
        src = part.at[p, rows(dz, lax.rem(y + dy, YN))]
        return remote(src, ysum.at[p, dz, dy], ry_s.at[p, k], ry_r.at[p, k], yto(dy))

    def rz(p, dz):
        return remote(zsend.at[p, dz], zsum.at[p, dz], rz_s.at[p, dz], rz_r.at[p, dz], zto(dz))

    def az(p, dz):
        return remote(dp.at[p, rows(0, y)], dp.at[p, rows(dz, y)], az_s.at[p, dz], az_r.at[p, dz], zto(dz))

    def ay(p, dz, dy):
        k = dz * 4 + dy
        here = dp.at[p, rows(dz, y)]
        return remote(here, here, ay_s.at[p, k], ay_r.at[p, k], yto(dy))

    def ay_arrival(p, dz, dy):
        k = dz * 4 + dy
        here = dp.at[p, rows(dz, lax.rem(y + 4 - dy, YN))]
        return remote(here, here, ay_s.at[p, k], ay_r.at[p, k], yto(dy))

    def ytotal(p, dz):
        t = part[p, rows(dz, y)].astype(F32)
        for dy in (1, 2, 3):
            ry(p, dz, dy).wait_recv()
        for dy in (1, 2, 3):
            t = t + ysum[p, dz, dy].astype(F32)
        return t

    def start_sums(p):
        for b in range(2):
            k = 2 * p + b
            remote(vol_hbm.at[1 - p], vbuf.at[3 * p, b], halo_s.at[k], halo_r.at[k], near(up, b)).wait_recv()
        inside = jnp.where(p == 0, slab, slabs - 1 - slab) > 0
        for b in range(2):
            columns(3 * p, b, inside)
        part[p] = (acc[p] + dot(wturn[p], cols[3 * p])).astype(BF)
        for dz in (3, 2, 1, 0):
            for dy in (2, 1, 3):
                ry(p, dz, dy).start()

    def pass_sums(p):
        for dz in (3, 2, 1):
            zsend[p, dz] = ytotal(p, dz).astype(BF)
            rz(p, dz).start()

    start_sums(first)
    cell = iota((HW, 128), 0)
    coarse = iota((HW, 128), 1)
    pool = (coarse == (cell // (2 * W)) * (W // 2) + (cell % W) // 2).astype(BF)
    cell = iota((128, HW), 1)
    coarse = iota((128, HW), 0)
    unpool = (coarse == (cell // (2 * W)) * (W // 2) + (cell % W) // 2).astype(BF)
    load_o.wait()
    load_c.wait()
    upper = dot(cot_ref[0], unpool) * 0.125
    diag = iota((16, 16), 0) == iota((16, 16), 1)
    offset = jnp.sum(jnp.where(diag, jnp.broadcast_to(off_ref[...], (16, 16)), 0.0), axis=1, keepdims=True)
    def activate(p):
        v = ytotal(p, 0) + offset
        for dz in (1, 2, 3):
            rz(p, dz).wait_recv()
            v = v + zsum[p, dz].astype(F32)
        s = jax.nn.sigmoid(v)
        dp[p, rows(0, y)] = (upper * s * (1.0 + v * (1.0 - s))).astype(BF)
        for dz in (3, 2, 1):
            az(p, dz).start()
        for dy in (2, 1, 3):
            ay(p, 0, dy).start()
        return v * s

    def forward(p):
        for dz in (1, 2, 3):
            az(p, dz).wait_recv()
            for dy in (2, 1, 3):
                ay(p, dz, dy).start()

    start_sums(second)
    pass_sums(first)
    pass_sums(second)
    act = activate(first)
    forward(first)
    act = act + activate(second)
    forward(second)
    act_hi = act.astype(BF)
    act_lo = (act - act_hi.astype(F32)).astype(BF)
    pooled_ref[0] = ((dot(act_hi, pool) + dot(act_lo, pool)) * 0.125).astype(BF)
    def gathered(prod):
        out = []
        for b in range(2):
            g = jnp.zeros((16, HW), F32)
            for kh in range(3):
                for kw in range(3):
                    row = b * 144 + (kh * 3 + kw) * 16
                    g = g + moved(prod[row : row + 16], 1 - kh, 1 - kw)
            out.append(g)
        return out

    def edge(p, b):
        slab_to = jnp.where(p == 0, down, up)
        return remote(
            hsend.at[p, b], hrecv.at[1 - p, b], bh_s.at[2 * p + b], bh_r.at[2 * (1 - p) + b], near(slab_to, b)
        )

    for p in planes:
        for dz in range(4):
            for dy in (1, 2, 3):
                ay_arrival(p, dz, dy).wait_recv()
        beyond = gathered(dot(wh[2 * p].reshape(288, 256), dp[p]))
        for b in range(2):
            hsend[p, b] = beyond[b].astype(BF)
            edge(p, b).start()
    flat = [wh[k].reshape(288, 256) for k in range(3)]
    dp0, dp1 = dp[0], dp[1]
    g0 = gathered(dot(flat[0], dp1) + dot(flat[1], dp0))
    g1 = gathered(dot(flat[1], dp1) + dot(flat[2], dp0))
    psend[0] = g0[1].astype(BF)
    psend[1] = g1[1].astype(BF)
    pair = remote(psend, precv, pair_s, pair_r, sib)
    pair.start()
    pair.wait_recv()
    g0 = g0[0] + precv[0].astype(F32)
    g1 = g1[0] + precv[1].astype(F32)
    for p in range(2):
        for b in range(2):
            edge(p, b).wait_recv()
    from_down = hrecv[0, 0].astype(F32) + hrecv[0, 1].astype(F32)
    from_up = hrecv[1, 0].astype(F32) + hrecv[1, 1].astype(F32)
    grad_ref[0] = (g0 + jnp.where(slab > 0, from_down, 0.0)).astype(BF)
    grad_ref[1] = (g1 + jnp.where(slab < slabs - 1, from_up, 0.0)).astype(BF)

    for c in halo + [share_v, share_w, pair]:
        c.wait_send()
    for p in range(2):
        for b in range(2):
            edge(p, b).wait_send()
        for dz in range(4):
            for dy in (1, 2, 3):
                ry(p, dz, dy).wait_send()
                ay(p, dz, dy).wait_send()
        for dz in (1, 2, 3):
            rz(p, dz).wait_send()
            az(p, dz).wait_send()


def per_device(volume, kernel, offset, cotangent):
    vmem = pl.BlockSpec(memory_space=pltpu.VMEM)
    hbm = pl.BlockSpec(memory_space=pl.ANY)
    dma = pltpu.SemaphoreType.DMA
    return pl.pallas_call(
        body,
        out_shape=(
            jax.ShapeDtypeStruct((1, 16, HW // 4), BF),
            jax.ShapeDtypeStruct((2, 16, HW), BF),
        ),
        in_specs=[hbm] * 4,
        out_specs=(vmem, vmem),
        scratch_shapes=[
            pltpu.VMEM((4, 2, 16, HW), BF),
            pltpu.VMEM((27, 16, 512), BF),
            pltpu.VMEM((2, 256, 288), BF),
            pltpu.VMEM((1, 16), F32),
            pltpu.VMEM((1, 16, HW // 4), BF),
            pltpu.VMEM((3, 144, 256), BF),
            pltpu.VMEM((3, 2, 144, 256), BF),
            pltpu.VMEM((4, 288, HW), BF),
            pltpu.VMEM((2, 256, HW), F32),
            pltpu.VMEM((2, 256, HW), BF),
            pltpu.VMEM((2, 4, 4, 16, HW), BF),
            pltpu.VMEM((2, 4, 16, HW), BF),
            pltpu.VMEM((2, 4, 16, HW), BF),
            pltpu.VMEM((2, 256, HW), BF),
            pltpu.VMEM((2, 2, 16, HW), BF),
            pltpu.VMEM((2, 2, 16, HW), BF),
            pltpu.VMEM((2, 16, HW), BF),
            pltpu.VMEM((2, 16, HW), BF),
            dma((4,)), dma((4,)), dma((4,)), dma((2,)), dma((2,)),
            dma((2, 16)), dma((2, 16)), dma((2, 4)), dma((2, 4)),
            dma((2, 4)), dma((2, 4)), dma((2, 16)), dma((2, 16)),
            dma((4,)), dma((4,)), dma, dma,
        ],
        compiler_params=pltpu.CompilerParams(
            collective_id=0, has_side_effects=True, vmem_limit_bytes=40 * 2**20
        ),
        name="conv_level",
    )(*(pltpu.with_memory_space_constraint(a, pltpu.HBM) for a in (volume, kernel, offset.reshape(1, 16), cotangent)))


def solution(mesh):
    return jax.shard_map(
        per_device,
        mesh=mesh,
        in_specs=(
            P("slab", "chan", None),
            P(None, "chan", None),
            P("chan"),
            P("slab", "chan", None),
        ),
        out_specs=(P("slab", "chan", None), P("slab", "chan", None)),
        check_vma=False,
    )
```

time: 52.7 us -> 50.2 us (0.953)
  Pallas kernels: 50.8 us -> 48.2 us
    pallas_call x1, Pallas kernels: 50.8 us -> 48.2 us  [per_device(): pl.pallas_call(body, out_shape=(jax.ShapeDtypeStruct((1, 16, HW // 4), BF...]
where the time goes in v3:
time: 50.2 us; the launch traced here: 50.1 us
  Pallas kernels  48.2 us (96%)
  local copies, waits for them, and re-layouts  1.21 us (2%)
  between operations  0.64 us (1%)
    pallas_call x1, Pallas kernels, per_device(): pl.pallas_call(body, out_shape=(jax.ShapeDtypeStruct((1, 16, HW // 4), BF...  48.2 us
    unnamed x2, local copies, waits for them, and re-layouts  1.21 us

profile of v3, /device:TPU:1, one launch (start us, length us, event | category | flops | bytes accessed | tf_op | source)
XLA Modules:
  0.0 50.1 jit_solution(5780949919447913290)
XLA Ops:
  0.6 48.2 %conv_level.1 = (bf16[1,16,128]{2,1,0:T(8,128)(2,1)S(1)}, bf16[2,16,512]{2,1,0:T(8,128)(2,1)S(1)}) custom-call(bf16[2,16,512]{2,1,0:T(8,128)(2,1)} %vol_hbm.1, bf16[27,16,512]{2,1,0:T(8,128)(2,1)} %w_hbm.1, f32[1,16]{1,0:T(1,128)} %bitcast.1, bf16[1,16,128]{2,1,0:T(8,128)(2,1)} %cot_hbm.1), custom_call_target="tpu_custom_call" | custom-call | tf_op jit(solution)/shard_map/conv_level/pallas_call | solution.py:295
  48.9 0.6 %copy.8 = bf16[1,16,128]{2,1,0:T(8,128)(2,1)} copy(bf16[1,16,128]{2,1,0:T(8,128)(2,1)S(1)} %get-tuple-element.4) | data formatting | bytes 8192
  49.5 0.6 %copy.9 = bf16[2,16,512]{2,1,0:T(8,128)(2,1)} copy(bf16[2,16,512]{2,1,0:T(8,128)(2,1)S(1)} %get-tuple-element.5) | data formatting | bytes 65536

commit v4 on v3

--- a/solution.py
+++ b/solution.py
@@ -72,9 +72,15 @@
 
     barrier = pltpu.get_barrier_semaphore()
     pl.semaphore_signal(barrier, inc=1, device_id=sib, device_id_type=MESH)
-    for s in (up, down):
-        for b in range(2):
-            pl.semaphore_signal(barrier, inc=1, device_id=near(s, b), device_id_type=MESH)
+    has_up = slab < slabs - 1
+    has_down = slab > 0
+    for s, has in ((up, has_up), (down, has_down)):
+
+        @pl.when(has)
+        def _():
+            for b in range(2):
+                pl.semaphore_signal(barrier, inc=1, device_id=near(s, b), device_id_type=MESH)
+
 
     for d in range(1, 4):
         pl.semaphore_signal(barrier, inc=1, device_id=zto(d), device_id_type=MESH)
@@ -88,14 +94,27 @@
     load_c = pltpu.make_async_copy(cot_hbm, cot_ref, lsem.at[3])
     load_o.start()
     load_c.start()
-    pl.semaphore_wait(barrier, 11)
-
-    halo = []
-    for b in range(2):
-        halo.append(remote(vol_hbm.at[1], vbuf.at[0, b], halo_s.at[b], halo_r.at[b], near(up, b)))
-        halo.append(remote(vol_hbm.at[0], vbuf.at[3, b], halo_s.at[2 + b], halo_r.at[2 + b], near(down, b)))
-    for c in halo:
-        c.start()
+    pl.semaphore_wait(barrier, 7 + 2 * has_up.astype(jnp.int32) + 2 * has_down.astype(jnp.int32))
+
+    def halo(p, b):
+        k = 2 * p + b
+        slab_to = jnp.where(p == 0, up, down)
+        return remote(vol_hbm.at[1 - p], vbuf.at[3 * p, b], halo_s.at[k], halo_r.at[k], near(slab_to, b))
+
+    def sends(p):
+        return jnp.where(p == 0, slabs - 1 - slab, slab) > 0
+
+    def receives(p):
+        return jnp.where(p == 0, slab, slabs - 1 - slab) > 0
+
+    def both(copy, p, act):
+        @pl.when(copy)
+        def _():
+            for b in range(2):
+                act(p, b)
+
+    for p in planes:
+        both(sends(p), p, lambda p, b: halo(p, b).start())
     share_v = remote(vol_hbm, vbuf.at[pl.ds(1, 2), 1], sib_s.at[0], sib_r.at[0], sib)
     share_w = remote(wsend, wh.at[:, 1], sib_s.at[1], sib_r.at[1], sib)
     share_v.start()
@@ -173,12 +192,9 @@
         return t
 
     def start_sums(p):
+        both(receives(p), p, lambda p, b: halo(p, b).wait_recv())
         for b in range(2):
-            k = 2 * p + b
-            remote(vol_hbm.at[1 - p], vbuf.at[3 * p, b], halo_s.at[k], halo_r.at[k], near(up, b)).wait_recv()
-        inside = jnp.where(p == 0, slab, slabs - 1 - slab) > 0
-        for b in range(2):
-            columns(3 * p, b, inside)
+            columns(3 * p, b, receives(p))
         part[p] = (acc[p] + dot(wturn[p], cols[3 * p])).astype(BF)
         for dz in (3, 2, 1, 0):
             for dy in (2, 1, 3):
@@ -214,8 +230,8 @@
             ay(p, 0, dy).start()
         return v * s
 
-    def forward(p):
-        for dz in (1, 2, 3):
+    def forward(p, dzs=(1, 2, 3)):
+        for dz in dzs:
             az(p, dz).wait_recv()
             for dy in (2, 1, 3):
                 ay(p, dz, dy).start()
@@ -224,12 +240,22 @@
     pass_sums(first)
     pass_sums(second)
     act = activate(first)
+    act = act + activate(second)
     forward(first)
-    act = act + activate(second)
     forward(second)
     act_hi = act.astype(BF)
     act_lo = (act - act_hi.astype(F32)).astype(BF)
     pooled_ref[0] = ((dot(act_hi, pool) + dot(act_lo, pool)) * 0.125).astype(BF)
+    share_v.wait_send()
+    share_w.wait_send()
+    for p in planes:
+        both(sends(p), p, lambda p, b: halo(p, b).wait_send())
+        for dz in range(4):
+            for dy in (1, 2, 3):
+                ry(p, dz, dy).wait_send()
+        for dz in (1, 2, 3):
+            rz(p, dz).wait_send()
+
     def gathered(prod):
         out = []
         for b in range(2):
@@ -254,7 +280,13 @@
         beyond = gathered(dot(wh[2 * p].reshape(288, 256), dp[p]))
         for b in range(2):
             hsend[p, b] = beyond[b].astype(BF)
-            edge(p, b).start()
+        both(receives(p), p, lambda p, b: edge(p, b).start())
+    for p in planes:
+        for dz in range(4):
+            for dy in (1, 2, 3):
+                ay(p, dz, dy).wait_send()
+        for dz in (1, 2, 3):
+            az(p, dz).wait_send()
     flat = [wh[k].reshape(288, 256) for k in range(3)]
     dp0, dp1 = dp[0], dp[1]
     g0 = gathered(dot(flat[0], dp1) + dot(flat[1], dp0))
@@ -266,26 +298,16 @@
     pair.wait_recv()
     g0 = g0[0] + precv[0].astype(F32)
     g1 = g1[0] + precv[1].astype(F32)
-    for p in range(2):
-        for b in range(2):
-            edge(p, b).wait_recv()
+    for p in planes:
+        both(sends(p), p, lambda p, b: edge(p, b).wait_recv())
     from_down = hrecv[0, 0].astype(F32) + hrecv[0, 1].astype(F32)
     from_up = hrecv[1, 0].astype(F32) + hrecv[1, 1].astype(F32)
     grad_ref[0] = (g0 + jnp.where(slab > 0, from_down, 0.0)).astype(BF)
     grad_ref[1] = (g1 + jnp.where(slab < slabs - 1, from_up, 0.0)).astype(BF)
 
-    for c in halo + [share_v, share_w, pair]:
-        c.wait_send()
-    for p in range(2):
-        for b in range(2):
-            edge(p, b).wait_send()
-        for dz in range(4):
-            for dy in (1, 2, 3):
-                ry(p, dz, dy).wait_send()
-                ay(p, dz, dy).wait_send()
-        for dz in (1, 2, 3):
-            rz(p, dz).wait_send()
-            az(p, dz).wait_send()
+    pair.wait_send()
+    for p in planes:
+        both(receives(p), p, lambda p, b: edge(p, b).wait_send())
 
 
 def per_device(volume, kernel, offset, cotangent):

time: 50.2 us -> 46.4 us (0.924)
  the two profiles are of different devices: /device:TPU:1 before, /device:TPU:7 now
where the time goes in v4:
time: 46.4 us; the launch traced here: 46.3 us
  Pallas kernels  44.4 us (96%)
  local copies, waits for them, and re-layouts  1.21 us (3%)
  between operations  0.64 us (1%)
    pallas_call x1, Pallas kernels, per_device(): pl.pallas_call(body, out_shape=(jax.ShapeDtypeStruct((1, 16, HW // 4), BF...  44.4 us
    unnamed x2, local copies, waits for them, and re-layouts  1.21 us

profile of v4, /device:TPU:7, one launch (start us, length us, event | category | flops | bytes accessed | tf_op | source)
XLA Modules:
  0.0 46.3 jit_solution(16233994763667835189)
XLA Ops:
  0.6 44.4 %conv_level.1 = (bf16[1,16,128]{2,1,0:T(8,128)(2,1)S(1)}, bf16[2,16,512]{2,1,0:T(8,128)(2,1)S(1)}) custom-call(bf16[2,16,512]{2,1,0:T(8,128)(2,1)} %vol_hbm.1, bf16[27,16,512]{2,1,0:T(8,128)(2,1)} %w_hbm.1, f32[1,16]{1,0:T(1,128)} %bitcast.1, bf16[1,16,128]{2,1,0:T(8,128)(2,1)} %cot_hbm.1), custom_call_target="tpu_custom_call" | custom-call | tf_op jit(solution)/shard_map/conv_level/pallas_call | solution.py:317
  45.1 0.6 %copy.8 = bf16[1,16,128]{2,1,0:T(8,128)(2,1)} copy(bf16[1,16,128]{2,1,0:T(8,128)(2,1)S(1)} %get-tuple-element.4) | data formatting | bytes 8192
  45.7 0.6 %copy.9 = bf16[2,16,512]{2,1,0:T(8,128)(2,1)} copy(bf16[2,16,512]{2,1,0:T(8,128)(2,1)S(1)} %get-tuple-element.5) | data formatting | bytes 65536

commit v5 on v4

--- a/solution.py
+++ b/solution.py
@@ -57,7 +57,7 @@
 
     zs = (z, z + 1 - 2 * lax.rem(z, 2), lax.rem(z + 2, 4), 3 - z)
 
-    first = lax.rem(slab, 4) // 3
+    first = lax.rem(slab, 4) // 2
     second = 1 - first
     planes = (first, second)
 
@@ -70,6 +70,8 @@
     def near(s, b):
         return (s, chan if b == 0 else chan + 1 - 2 * core)
 
+    load_v = pltpu.make_async_copy(vol_hbm, vbuf.at[pl.ds(1, 2), 0], lsem.at[0])
+    load_v.start()
     barrier = pltpu.get_barrier_semaphore()
     pl.semaphore_signal(barrier, inc=1, device_id=sib, device_id_type=MESH)
     has_up = slab < slabs - 1
@@ -86,9 +88,7 @@
         pl.semaphore_signal(barrier, inc=1, device_id=zto(d), device_id_type=MESH)
         pl.semaphore_signal(barrier, inc=1, device_id=yto(d), device_id_type=MESH)
 
-    load_v = pltpu.make_async_copy(vol_hbm, vbuf.at[pl.ds(1, 2), 0], lsem.at[0])
     load_w = pltpu.make_async_copy(w_hbm, wraw, lsem.at[1])
-    load_v.start()
     load_w.start()
     load_o = pltpu.make_async_copy(off_hbm, off_ref, lsem.at[2])
     load_c = pltpu.make_async_copy(cot_hbm, cot_ref, lsem.at[3])
@@ -96,10 +96,12 @@
     load_c.start()
     pl.semaphore_wait(barrier, 7 + 2 * has_up.astype(jnp.int32) + 2 * has_down.astype(jnp.int32))
 
+    load_v.wait()
+
     def halo(p, b):
         k = 2 * p + b
         slab_to = jnp.where(p == 0, up, down)
-        return remote(vol_hbm.at[1 - p], vbuf.at[3 * p, b], halo_s.at[k], halo_r.at[k], near(slab_to, b))
+        return remote(vbuf.at[2 - p, 0], vbuf.at[3 * p, b], halo_s.at[k], halo_r.at[k], near(slab_to, b))
 
     def sends(p):
         return jnp.where(p == 0, slabs - 1 - slab, slab) > 0
@@ -128,8 +130,6 @@
     wsend[...] = dot(wflat, (place == 16 * (1 - core)).astype(BF)).astype(BF).reshape(3, 144, 256)
     share_w.start()
     wh[:, 0] = dot(wflat, (place == 16 * core).astype(BF)).astype(BF).reshape(3, 144, 256)
-    load_v.wait()
-
     def columns(plane, b, keep=None):
         x = vbuf[plane, b].astype(F32)
         if keep is not None:

time: 46.4 us -> 45.8 us (0.987)
  Pallas kernels: 44.4 us -> 43.9 us
    pallas_call x1, Pallas kernels: 44.4 us -> 43.9 us  [per_device(): pl.pallas_call(body, out_shape=(jax.ShapeDtypeStruct((1, 16, HW // 4), BF...]
where the time goes in v5:
time: 45.8 us; the launch traced here: 45.7 us
  Pallas kernels  43.9 us (96%)
  local copies, waits for them, and re-layouts  1.21 us (3%)
  between operations  0.64 us (1%)
    pallas_call x1, Pallas kernels, per_device(): pl.pallas_call(body, out_shape=(jax.ShapeDtypeStruct((1, 16, HW // 4), BF...  43.9 us
    unnamed x2, local copies, waits for them, and re-layouts  1.21 us

profile of v5, /device:TPU:7, one launch (start us, length us, event | category | flops | bytes accessed | tf_op | source)
XLA Modules:
  0.0 45.7 jit_solution(10575413793724301947)
XLA Ops:
  0.6 43.9 %conv_level.1 = (bf16[1,16,128]{2,1,0:T(8,128)(2,1)S(1)}, bf16[2,16,512]{2,1,0:T(8,128)(2,1)S(1)}) custom-call(bf16[2,16,512]{2,1,0:T(8,128)(2,1)} %vol_hbm.1, bf16[27,16,512]{2,1,0:T(8,128)(2,1)} %w_hbm.1, f32[1,16]{1,0:T(1,128)} %bitcast.1, bf16[1,16,128]{2,1,0:T(8,128)(2,1)} %cot_hbm.1), custom_call_target="tpu_custom_call" | custom-call | tf_op jit(solution)/shard_map/conv_level/pallas_call | solution.py:317
  44.5 0.6 %copy.8 = bf16[1,16,128]{2,1,0:T(8,128)(2,1)} copy(bf16[1,16,128]{2,1,0:T(8,128)(2,1)S(1)} %get-tuple-element.4) | data formatting | bytes 8192
  45.1 0.6 %copy.9 = bf16[2,16,512]{2,1,0:T(8,128)(2,1)} copy(bf16[2,16,512]{2,1,0:T(8,128)(2,1)S(1)} %get-tuple-element.5) | data formatting | bytes 65536

commit v6 on v5

--- a/solution.py
+++ b/solution.py
@@ -192,8 +192,12 @@
         return t
 
     def start_sums(p):
-        both(receives(p), p, lambda p, b: halo(p, b).wait_recv())
         for b in range(2):
+
+            @pl.when(receives(p))
+            def _():
+                halo(p, b).wait_recv()
+
             columns(3 * p, b, receives(p))
         part[p] = (acc[p] + dot(wturn[p], cols[3 * p])).astype(BF)
         for dz in (3, 2, 1, 0):

time: 45.8 us -> 46.3 us (1.011)
  the two profiles are of different devices: /device:TPU:7 before, /device:TPU:5 now
where the time goes in v6:
time: 46.3 us; the launch traced here: 46.2 us
  Pallas kernels  44.4 us (96%)
  local copies, waits for them, and re-layouts  1.21 us (3%)
  between operations  0.64 us (1%)
    pallas_call x1, Pallas kernels, per_device(): pl.pallas_call(body, out_shape=(jax.ShapeDtypeStruct((1, 16, HW // 4), BF...  44.4 us
    unnamed x2, local copies, waits for them, and re-layouts  1.21 us

profile of v6, /device:TPU:5, one launch (start us, length us, event | category | flops | bytes accessed | tf_op | source)
XLA Modules:
  0.0 46.2 jit_solution(4515592862711497498)
XLA Ops:
  0.6 44.4 %conv_level.1 = (bf16[1,16,128]{2,1,0:T(8,128)(2,1)S(1)}, bf16[2,16,512]{2,1,0:T(8,128)(2,1)S(1)}) custom-call(bf16[2,16,512]{2,1,0:T(8,128)(2,1)} %vol_hbm.1, bf16[27,16,512]{2,1,0:T(8,128)(2,1)} %w_hbm.1, f32[1,16]{1,0:T(1,128)} %bitcast.1, bf16[1,16,128]{2,1,0:T(8,128)(2,1)} %cot_hbm.1), custom_call_target="tpu_custom_call" | custom-call | tf_op jit(solution)/shard_map/conv_level/pallas_call | solution.py:321
  45.0 0.6 %copy.8 = bf16[1,16,128]{2,1,0:T(8,128)(2,1)} copy(bf16[1,16,128]{2,1,0:T(8,128)(2,1)S(1)} %get-tuple-element.4) | data formatting | bytes 8192
  45.6 0.6 %copy.9 = bf16[2,16,512]{2,1,0:T(8,128)(2,1)} copy(bf16[2,16,512]{2,1,0:T(8,128)(2,1)S(1)} %get-tuple-element.5) | data formatting | bytes 65536
